TPU v7x, 256 devices: a whole 4x4x8 slice. The times are simulated.
256 devices in a mesh: rx: 16 (over z, y_lo), ry: 4 (over x), ma: 4 (over y_hi, core).
Axes of the slice: x: 4, y: 4 (y_hi: 2, y_lo: 2; y = y_hi * 2 + y_lo), z: 8, core: 2. Of those that a mesh axis runs over, the one named last changes fastest.
Arguments:
- numerator: float32 [16, 4, 120, 13824], P('rx', 'ry', None, 'ma'), may hold values from -6 to 6
- weight: float32 [16, 4], P('rx', 'ry'), may hold values from 0.5 to 2
- inputs: bfloat16 [16, 4, 2, 256, 13824], P('rx', 'ry', None, None, 'ma'), may hold values from -0.125 to 0.125
- targets: float32 [16, 4, 2, 120, 256], P('rx', 'ry'), may hold values from -6 to 6
- first_moment: float32 [16, 4, 120, 13824], P('rx', 'ry', None, 'ma'), may hold values from -1.5 to 1.5
- second_moment: float32 [16, 4, 120, 13824], P('rx', 'ry', None, 'ma'), may hold values from 0.005 to 0.2
Outputs:
- new_numerator: float32 [16, 4, 120, 13824], P('rx', 'ry', None, 'ma')
- new_weight: float32 [16, 4], P('rx', 'ry')
- new_first: float32 [16, 4, 120, 13824], P('rx', 'ry', None, 'ma')
- new_second: float32 [16, 4, 120, 13824], P('rx', 'ry', None, 'ma')
All inputs are finite; a program needn't handle non-finite values.
Results may differ from a plain program's by a relative error of at most 0.0003.
Values sent between devices are 32-bit elements; how exact they have to be, the bound alone decides.
No kernel may reach another device: no remote copies, remote signals or barrier semaphores. Data moves between devices by JAX's collectives and lax.ppermute only.
A program may use at most 64 MiB of HBM per device.

v0:
```python
import jax
import jax.numpy as jnp
from jax import lax
from jax.sharding import PartitionSpec as P

PRIOR_STEPS = 100
BETA_ONE = 0.9
BETA_TWO = 0.999
LEARN_RATE = 0.05
EPSILON = 1e-08


def shifted(block, axis, distance):
    devices = range(lax.axis_size(axis))
    route = [((i - distance) % len(devices), i) for i in devices]
    return lax.ppermute(block, axis, route)


def adam_update(params, gradient, first, second, count):
    first = BETA_ONE * first + (1.0 - BETA_ONE) * gradient
    second = BETA_TWO * second + (1.0 - BETA_TWO) * gradient * gradient
    first_corr = 1.0 - BETA_ONE**count
    second_corr = 1.0 - BETA_TWO**count
    params = params - LEARN_RATE * (first / first_corr) / (jnp.sqrt(second / second_corr) + EPSILON)
    return (params, first, second)


def mix_row(values, scales):
    left_values, left_scales = shifted((values, scales), "rx", 1)
    right_values, right_scales = shifted((values, scales), "rx", -1)
    return (
        (values + left_values + right_values) / 3.0,
        (scales + left_scales + right_scales) / 3.0,
    )


def mix_column(values, scales):
    left_values, left_scales = shifted((values, scales), "ry", 1)
    right_values, right_scales = shifted((values, scales), "ry", -1)
    return (
        (values + left_values + right_values) / 3.0,
        (scales + left_scales + right_scales) / 3.0,
    )


def one_round(values, scales, first, second, inputs_narrow, targets_round, mixer, count):
    inputs_round = inputs_narrow.astype(jnp.float32)
    values, scales = mixer(values, scales)
    params = values[0, 0] / scales[0, 0]
    partial_pred = jnp.einsum("cf,tf->ct", params, inputs_round, precision=lax.Precision.HIGHEST)
    predicted = lax.psum(partial_pred, "ma")
    gradient = jnp.einsum(
        "ct,tf->cf", predicted - targets_round, inputs_round, precision=lax.Precision.HIGHEST
    )
    params, new_first, new_second = adam_update(params, gradient, first[0, 0], second[0, 0], count)
    values = (scales[0, 0] * params)[None, None]
    return (values, scales, new_first[None, None], new_second[None, None])


def local(numerator, weight, inputs, targets, first_moment, second_moment):
    values, scales, first, second = one_round(
        numerator,
        weight,
        first_moment,
        second_moment,
        inputs[0, 0, 0],
        targets[0, 0, 0],
        mix_row,
        PRIOR_STEPS + 1,
    )
    values, scales, first, second = one_round(
        values,
        scales,
        first,
        second,
        inputs[0, 0, 1],
        targets[0, 0, 1],
        mix_column,
        PRIOR_STEPS + 2,
    )
    return (values, scales, first, second)


def solution(mesh):
    return jax.shard_map(
        local,
        mesh=mesh,
        in_specs=(
            P("rx", "ry", None, "ma"),
            P("rx", "ry"),
            P("rx", "ry", None, None, "ma"),
            P("rx", "ry", None, None, None),
            P("rx", "ry", None, "ma"),
            P("rx", "ry", None, "ma"),
        ),
        out_specs=(
            P("rx", "ry", None, "ma"),
            P("rx", "ry"),
            P("rx", "ry", None, "ma"),
            P("rx", "ry", None, "ma"),
        ),
        check_vma=False,
    )
```

profile of v0, /device:TPU:1, one launch (start us, length us, event | category | flops | bytes accessed | tf_op | source)
XLA Modules:
  0.0 253.2 jit_solution(13335298537395719774)
XLA Ops:
  7.2 0.0 all-reduce.3.cloned.1.call-start
  7.2 2.2 collective-permute-start.4
  9.4 5.4 %collective-permute-start.5 = (f32[1,1,120,3456]{3,2,1,0:T(8,128)}, f32[1,1,120,3456]{3,2,1,0:T(8,128)S(1)}, u32[]{:S(2)}, u32[]{:S(2)}) collective-permute-start(f32[1,1,120,3456]{3,2,1,0:T(8,128)} %param.6), channel_id=1, source_target_pairs={{16,0},{32,16},{48,32},{64,48},{80,64},{96,80},{112,96},{128,112},... | collective-permute-start | bytes 4976648 | tf_op jit(solution)/shard_map/ppermute | solution.py:16
  14.8 0.0 collective-permute-start
  14.8 3.6 %collective-permute-start.1 = (f32[1,1]{1,0:T(1,128)}, f32[1,1]{1,0:T(1,128)}, u32[]{:S(2)}, u32[]{:S(2)}) collective-permute-start(f32[1,1]{1,0:T(1,128)} %param.7), channel_id=1, source_target_pairs={{16,0},{32,16},{48,32},{64,48},{80,64},{96,80},{112,96},{128,112},... | collective-permute-start | bytes 20 | tf_op jit(solution)/shard_map/ppermute | solution.py:16
  19.1 60.9 %collective-permute-done = f32[1,1]{1,0:T(1,128)} collective-permute-done((f32[1,1]{1,0:T(1,128)}, f32[1,1]{1,0:T(1,128)}, u32[]{:S(2)}, u32[]{:S(2)}) %collective-permute-start) | collective-permute-done | bytes 36 | tf_op jit(solution)/shard_map/ppermute | solution.py:16
  80.6 1.3 collective-permute-done.1
  82.6 0.0 collective-permute-done.4
  82.6 0.0 copy-start.3
  82.6 0.0 copy-start.4
  82.6 1.1 copy-done.3
  83.8 0.5 copy-done.4
  84.3 4.4 %fusion.6 = f32[120,256]{1,0:T(8,128)} fusion(bf16[1,1,2,256,3456]{4,3,2,1,0:T(8,128)(2,1)} %param.8, f32[1,1,120,3456]{3,2,1,0:T(8,128)S(1)} %collective-permute-done.5, f32[1,1,120,3456]{3,2,1,0:T(8,128)} %param.6, f32[1,1,120,3456]{3,2,1,0:T(8,128)S(1)} %collective-permute-done.4, f32[]{:T(128)} %bitcast.1), kind=kOutput, calls=%fused_computation.8 | convolution fusion | flops 1275678720 | bytes 6869504 | tf_op jit(solution)/shard_map/cf,tf->ct/dot_general | solution.py:50
  88.7 0.0 all-reduce.3.cloned.1.call-update
  88.8 0.0 copy-start
  88.8 0.0 all-reduce.5.cloned.1.call-start
  88.8 49.7 %all-reduce.3.cloned.1.call-done = f32[120,256]{1,0:T(8,128)} async-done(((f32[120,256]{1,0:T(8,128)}), f32[120,256]{1,0:T(8,128)}) %all-reduce.3.cloned.1.call-update) | async-done | bytes 122896 | tf_op jit(solution)/shard_map/psum | solution.py:51
  138.6 2.5 fusion.4
  141.1 0.0 copy-start.5
  141.1 4.5 %fusion.15 = f32[1,1,120,3456]{3,2,1,0:T(8,128)S(1)} fusion(f32[]{:T(128)} %bitcast.1, f32[120,3456]{1,0:T(8,128)S(1)} %fusion.4, f32[1,1,120,3456]{3,2,1,0:T(8,128)} %param.10, f32[1,1,120,3456]{3,2,1,0:T(8,128)} %param.11, f32[1,1,120,3456]{3,2,1,0:T(8,128)} %copy-done.4, f32[1,1,120,3456]{3,2,1,0:T(8,128)S(1)} %copy-done, f32[1,1,120,3456]{3,2,1,0:T(8,128)} %copy-done.3), kind=kLoop, calls=%fused_computation.20 | loop fusion | flops 7050240 | bytes 11612164 | tf_op jit(solution)/shard_map/broadcast_in_dim | solution.py:56
  145.6 2.5 collective-permute-start.7
  148.1 35.5 %collective-permute-start.3 = (f32[1,1]{1,0:T(1,128)}, f32[1,1]{1,0:T(1,128)}, u32[]{:S(2)}, u32[]{:S(2)}) collective-permute-start(f32[1,1]{1,0:T(1,128)} %div.50), channel_id=1, source_target_pairs={{4,0},{8,4},{12,8},{0,12},{5,1},{9,5},{13,9},{1,13},{6,2},{10,6},{... | collective-permute-start | bytes 20 | tf_op jit(solution)/shard_map/ppermute | solution.py:16
  183.6 0.7 collective-permute-start.2
  184.3 3.2 %collective-permute-done.2 = f32[1,1]{1,0:T(1,128)} collective-permute-done((f32[1,1]{1,0:T(1,128)}, f32[1,1]{1,0:T(1,128)}, u32[]{:S(2)}, u32[]{:S(2)}) %collective-permute-start.2) | collective-permute-done | bytes 36 | tf_op jit(solution)/shard_map/ppermute | solution.py:16
  188.8 0.0 copy-start.6
  188.8 0.0 copy-start.7
  188.8 1.1 copy-done.6
  190.0 0.5 copy-done.7
  190.5 2.4 fusion.2
  192.9 0.0 all-reduce.5.cloned.1.call-update
  193.0 43.8 %all-reduce.5.cloned.1.call-done = f32[120,256]{1,0:T(8,128)} async-done(((f32[120,256]{1,0:T(8,128)}), f32[120,256]{1,0:T(8,128)}) %all-reduce.5.cloned.1.call-update) | async-done | bytes 122896 | tf_op jit(solution)/shard_map/psum | solution.py:51
  236.8 8.4 %fusion.21 = (f32[1,1,120,3456]{3,2,1,0:T(8,128)}, f32[1,1,120,3456]{3,2,1,0:T(8,128)}, f32[1,1,120,3456]{3,2,1,0:T(8,128)}) fusion(f32[120,3456]{1,0:T(8,128)S(1)} %fusion.4, f32[1,1,120,3456]{3,2,1,0:T(8,128)S(1)} %copy-done.1, f32[1,1,120,3456]{3,2,1,0:T(8,128)} %param.10, f32[]{:T(128)} %bitcast, f32[1,1,120,3456]{3,2,1,0:T(8,128)} %copy-done.6, ...), kind=kOutput, calls=%fused_computation.29 | convolution fusion | flops 1284003840 | bytes 16946176 | tf_op jit(solution)/shard_map/ct,tf->cf/dot_general | solution.py:52
  (11 shorter events, 0.0 us)
Async XLA Ops:
  7.2 131.4 %all-reduce.3.cloned.1.call-start = ((), (), s32[]{:S(2)}) async-start(), calls=%async_computation | async-start | bytes 245760 | tf_op jit(solution)/shard_map/psum | solution.py:51
  7.2 75.4 %collective-permute-start.4 = (f32[1,1,120,3456]{3,2,1,0:T(8,128)}, f32[1,1,120,3456]{3,2,1,0:T(8,128)S(1)}, u32[]{:S(2)}, u32[]{:S(2)}) collective-permute-start(f32[1,1,120,3456]{3,2,1,0:T(8,128)} %param.6), channel_id=1, source_target_pairs={{240,0},{0,16},{16,32},{32,48},{48,64},{64,80},{80,96},{96,112},{1... | collective-permute-start | bytes 4976648 | tf_op jit(solution)/shard_map/ppermute | solution.py:16
  9.4 73.2 %collective-permute-start.5 = (f32[1,1,120,3456]{3,2,1,0:T(8,128)}, f32[1,1,120,3456]{3,2,1,0:T(8,128)S(1)}, u32[]{:S(2)}, u32[]{:S(2)}) collective-permute-start(f32[1,1,120,3456]{3,2,1,0:T(8,128)} %param.6), channel_id=1, source_target_pairs={{16,0},{32,16},{48,32},{64,48},{80,64},{96,80},{112,96},{128,112},... | collective-permute-start | bytes 4976648 | tf_op jit(solution)/shard_map/ppermute | solution.py:16
  14.8 65.2 %collective-permute-start = (f32[1,1]{1,0:T(1,128)}, f32[1,1]{1,0:T(1,128)}, u32[]{:S(2)}, u32[]{:S(2)}) collective-permute-start(f32[1,1]{1,0:T(1,128)} %param.7), channel_id=1, source_target_pairs={{240,0},{0,16},{16,32},{32,48},{48,64},{64,80},{80,96},{96,112},{1... | collective-permute-start | bytes 20 | tf_op jit(solution)/shard_map/ppermute | solution.py:16
  14.8 67.1 %collective-permute-start.1 = (f32[1,1]{1,0:T(1,128)}, f32[1,1]{1,0:T(1,128)}, u32[]{:S(2)}, u32[]{:S(2)}) collective-permute-start(f32[1,1]{1,0:T(1,128)} %param.7), channel_id=1, source_target_pairs={{16,0},{32,16},{48,32},{64,48},{80,64},{96,80},{112,96},{128,112},... | collective-permute-start | bytes 20 | tf_op jit(solution)/shard_map/ppermute | solution.py:16
  82.6 1.2 copy-start.3
  82.6 1.7 copy-start.4
  88.8 52.3 %copy-start = (f32[1,1,120,3456]{3,2,1,0:T(8,128)S(1)}, f32[1,1,120,3456]{3,2,1,0:T(8,128)}, u32[]{:S(2)}) copy-start(f32[1,1,120,3456]{3,2,1,0:T(8,128)} %param.6) | copy-start | bytes 4976644
  88.8 148.0 %all-reduce.5.cloned.1.call-start = ((), (), s32[]{:S(2)}) async-start(), calls=%async_computation.1 | async-start | bytes 245760 | tf_op jit(solution)/shard_map/psum | solution.py:51
  141.1 49.4 %copy-start.5 = (bf16[1,1,2,256,3456]{4,3,2,1,0:T(8,128)(2,1)S(1)}, bf16[1,1,2,256,3456]{4,3,2,1,0:T(8,128)(2,1)}, u32[]{:S(2)}) copy-start(bf16[1,1,2,256,3456]{4,3,2,1,0:T(8,128)(2,1)} %param.8) | copy-start | bytes 10616836
  145.6 43.2 %copy-start.2 = (f32[1,1,120,3456]{3,2,1,0:T(8,128)}, f32[1,1,120,3456]{3,2,1,0:T(8,128)S(1)}, u32[]{:S(2)}) copy-start(f32[1,1,120,3456]{3,2,1,0:T(8,128)S(1)} %fusion.15) | copy-start | bytes 4976644
  145.6 43.2 %collective-permute-start.7 = (f32[1,1,120,3456]{3,2,1,0:T(8,128)S(1)}, f32[1,1,120,3456]{3,2,1,0:T(8,128)S(1)}, u32[]{:S(2)}, u32[]{:S(2)}) collective-permute-start(f32[1,1,120,3456]{3,2,1,0:T(8,128)S(1)} %fusion.15), channel_id=1, source_target_pairs={{4,0},{8,4},{12,8},{0,12},{5,1},{9,5},{13,9},{1,13},{6,2},{10,6},{... | collective-permute-start | bytes 4976648 | tf_op jit(solution)/shard_map/ppermute | solution.py:16
  148.1 40.7 %collective-permute-start.6 = (f32[1,1,120,3456]{3,2,1,0:T(8,128)S(1)}, f32[1,1,120,3456]{3,2,1,0:T(8,128)S(1)}, u32[]{:S(2)}, u32[]{:S(2)}) collective-permute-start(f32[1,1,120,3456]{3,2,1,0:T(8,128)S(1)} %fusion.15), channel_id=1, source_target_pairs={{12,0},{0,4},{4,8},{8,12},{13,1},{1,5},{5,9},{9,13},{14,2},{2,6},{... | collective-permute-start | bytes 4976648 | tf_op jit(solution)/shard_map/ppermute | solution.py:16
  148.1 40.1 %collective-permute-start.3 = (f32[1,1]{1,0:T(1,128)}, f32[1,1]{1,0:T(1,128)}, u32[]{:S(2)}, u32[]{:S(2)}) collective-permute-start(f32[1,1]{1,0:T(1,128)} %div.50), channel_id=1, source_target_pairs={{4,0},{8,4},{12,8},{0,12},{5,1},{9,5},{13,9},{1,13},{6,2},{10,6},{... | collective-permute-start | bytes 20 | tf_op jit(solution)/shard_map/ppermute | solution.py:16
  183.6 3.9 %collective-permute-start.2 = (f32[1,1]{1,0:T(1,128)}, f32[1,1]{1,0:T(1,128)}, u32[]{:S(2)}, u32[]{:S(2)}) collective-permute-start(f32[1,1]{1,0:T(1,128)} %div.50), channel_id=1, source_target_pairs={{12,0},{0,4},{4,8},{8,12},{13,1},{1,5},{5,9},{9,13},{14,2},{2,6},{... | collective-permute-start | bytes 20 | tf_op jit(solution)/shard_map/ppermute | solution.py:16
  188.8 1.2 copy-start.6
  188.8 1.7 copy-start.7
  190.5 46.3 %copy-start.1 = (f32[1,1,120,3456]{3,2,1,0:T(8,128)S(1)}, f32[1,1,120,3456]{3,2,1,0:T(8,128)}, u32[]{:S(2)}) copy-start(f32[1,1,120,3456]{3,2,1,0:T(8,128)} %param.11) | copy-start | bytes 4976644
Sparse Core Ops, SparseCore 0:
  88.9 49.6 all-reduce.2
  193.1 43.6 all-reduce.4
where the time goes:
time: 253 us
  waiting for transfers between devices  159 us (63%)
  starting transfers between devices  50 us (20%)
  between operations  18.5 us (7%)
  matrix products  17.7 us (7%)
  other arithmetic  4.47 us (2%)
  local copies, waits for them, and re-layouts  3.39 us (1%)
    psum x2, waiting for transfers between devices, one_round(): predicted = lax.psum(partial_pred, 'ma')  93.6 us
    ppermute x8, waiting for transfers between devices, shifted(): return lax.ppermute(block, axis, route)  65.5 us
    ppermute x8, starting transfers between devices, shifted(): return lax.ppermute(block, axis, route)  49.9 us
    dot_general x2, matrix products, one_round(): jnp.einsum('ct,tf->cf', predicted - targets_round, inputs_round, precisio...  10.9 us
    dot_general x2, matrix products, one_round(): jnp.einsum('cf,tf->ct', params, inputs_round, precision=lax.Precision.HIG...  6.85 us
  transfers between devices with their start and end apart: 10, of which 5 were waited for; matrix products, arithmetic and copies ran while one was open for 0% of the time, Pallas kernels for 0%

commit v1 on v0

--- a/solution.py
+++ b/solution.py
@@ -48,7 +48,12 @@
     values, scales = mixer(values, scales)
     params = values[0, 0] / scales[0, 0]
     partial_pred = jnp.einsum("cf,tf->ct", params, inputs_round, precision=lax.Precision.HIGHEST)
-    predicted = lax.psum(partial_pred, "ma")
+
+    def rest_signs_all(inner_x):
+        work_now = jax.lax.all_gather(inner_x, "ma")
+        return jnp.sum(work_now, axis=0)
+
+    predicted = rest_signs_all(partial_pred)
     gradient = jnp.einsum(
         "ct,tf->cf", predicted - targets_round, inputs_round, precision=lax.Precision.HIGHEST
     )

time: 253 us -> 163 us (0.64)
  waiting for transfers between devices: 159 us -> 65.5 us
  blocking collectives: 0 us -> 20.3 us
  between operations: 18.5 us -> 5.08 us
  local copies, waits for them, and re-layouts: 3.39 us -> 0.06 us
    psum x2 -> x0, waiting for transfers between devices: 93.6 us -> none  [one_round(): predicted = lax.psum(partial_pred, 'ma')]
    all_gather x0 -> x2, blocking collectives: none -> 20.3 us  [rest_signs_all(): work_now = jax.lax.all_gather(inner_x, 'ma')]
    unnamed x16 -> x20, local copies, waits for them, and re-layouts: 3.39 us -> 0.06 us
  transfers between devices with their start and end apart: 10 -> 8, of which waited for: 5 -> 3; matrix products, arithmetic and copies ran while one was open for 0% -> 0% of each run, Pallas kernels for 0% -> 0%
where the time goes in v1:
time: 163 us
  waiting for transfers between devices  65.5 us (40%)
  starting transfers between devices  50 us (31%)
  blocking collectives  20.3 us (12%)
  matrix products  18.1 us (11%)
  between operations  5.08 us (3%)
  other arithmetic  3.57 us (2%)
    ppermute x8, waiting for transfers between devices, shifted(): return lax.ppermute(block, axis, route)  65.5 us
    ppermute x8, starting transfers between devices, shifted(): return lax.ppermute(block, axis, route)  50 us
    all_gather x2, blocking collectives, rest_signs_all(): work_now = jax.lax.all_gather(inner_x, 'ma')  20.3 us
    dot_general x2, matrix products, one_round(): jnp.einsum('ct,tf->cf', predicted - targets_round, inputs_round, precisio...  11.3 us
    dot_general x2, matrix products, one_round(): jnp.einsum('cf,tf->ct', params, inputs_round, precision=lax.Precision.HIG...  6.78 us
    broadcast_in_dim x1, other arithmetic, one_round(): values = (scales[0, 0] * params)[None, None]  3.51 us
  transfers between devices with their start and end apart: 8, of which 3 were waited for; matrix products, arithmetic and copies ran while one was open for 0% of the time, Pallas kernels for 0%

profile of v1, /device:TPU:1, one launch (start us, length us, event | category | flops | bytes accessed | tf_op | source)
XLA Modules:
  0.0 162.5 jit_solution(1620925597276284029)
XLA Ops:
  0.6 2.2 %collective-permute-start.4 = (f32[1,1,120,3456]{3,2,1,0:T(8,128)}, f32[1,1,120,3456]{3,2,1,0:T(8,128)S(1)}, u32[]{:S(2)}, u32[]{:S(2)}) collective-permute-start(f32[1,1,120,3456]{3,2,1,0:T(8,128)} %param.6), channel_id=1, source_target_pairs={{240,0},{0,16},{16,32},{32,48},{48,64},{64,80},{80,96},{96,112},{1... | collective-permute-start | bytes 4976648 | tf_op jit(solution)/shard_map/ppermute | solution.py:16
  2.8 5.4 %collective-permute-start.5 = (f32[1,1,120,3456]{3,2,1,0:T(8,128)}, f32[1,1,120,3456]{3,2,1,0:T(8,128)S(1)}, u32[]{:S(2)}, u32[]{:S(2)}) collective-permute-start(f32[1,1,120,3456]{3,2,1,0:T(8,128)} %param.6), channel_id=1, source_target_pairs={{16,0},{32,16},{48,32},{64,48},{80,64},{96,80},{112,96},{128,112},... | collective-permute-start | bytes 4976648 | tf_op jit(solution)/shard_map/ppermute | solution.py:16
  8.2 0.0 collective-permute-start
  8.2 3.6 %collective-permute-start.1 = (f32[1,1]{1,0:T(1,128)}, f32[1,1]{1,0:T(1,128)}, u32[]{:S(2)}, u32[]{:S(2)}) collective-permute-start(f32[1,1]{1,0:T(1,128)} %param.7), channel_id=1, source_target_pairs={{16,0},{32,16},{48,32},{64,48},{80,64},{96,80},{112,96},{128,112},... | collective-permute-start | bytes 20 | tf_op jit(solution)/shard_map/ppermute | solution.py:16
  12.5 60.9 %collective-permute-done = f32[1,1]{1,0:T(1,128)} collective-permute-done((f32[1,1]{1,0:T(1,128)}, f32[1,1]{1,0:T(1,128)}, u32[]{:S(2)}, u32[]{:S(2)}) %collective-permute-start) | collective-permute-done | bytes 36 | tf_op jit(solution)/shard_map/ppermute | solution.py:16
  74.0 1.3 collective-permute-done.1
  76.0 0.0 collective-permute-done.4
  76.0 0.0 copy-start.4
  76.0 0.0 collective-permute-done.5
  76.0 0.0 copy-start.5
  76.0 0.0 copy-start.2
  76.0 5.0 %fusion.6 = f32[120,256]{1,0:T(8,128)S(1)} fusion(bf16[1,1,2,256,3456]{4,3,2,1,0:T(8,128)(2,1)} %param.8, f32[1,1,120,3456]{3,2,1,0:T(8,128)S(1)} %collective-permute-done.5, f32[1,1,120,3456]{3,2,1,0:T(8,128)} %param.6, f32[1,1,120,3456]{3,2,1,0:T(8,128)S(1)} %collective-permute-done.4, f32[]{:T(128)} %bitcast.1), kind=kOutput, calls=%fused_computation.8 | convolution fusion | flops 1275678720 | bytes 6869504 | tf_op jit(solution)/shard_map/cf,tf->ct/dot_general | solution.py:50
  81.0 10.6 %all-gather = f32[480,256]{1,0:T(8,128)S(1)} all-gather(f32[120,256]{1,0:T(8,128)S(1)} %fusion.6), channel_id=2, replica_groups=mesh['rx'=16,'ry'=4,'ma'=4] {'ma'}, dimensions={0}, use_global_device_ids=true | all-gather | bytes 614400 | tf_op jit(solution)/shard_map/all_gather | solution.py:53
  91.6 0.0 copy-start
  91.7 0.0 copy-start.1
  91.7 2.6 %fusion.4 = f32[120,3456]{1,0:T(8,128)S(1)} fusion(bf16[1,1,2,256,3456]{4,3,2,1,0:T(8,128)(2,1)} %param.8, f32[120,256]{1,0:T(8,128)S(1)} %reduce_sum.22, f32[1,1,2,120,256]{4,3,2,1,0:T(8,128)} %param.9), kind=kOutput, calls=%fused_computation.6 | convolution fusion | flops 1274050560 | bytes 3674112 | tf_op jit(solution)/shard_map/ct,tf->cf/dot_general | solution.py:57
  94.3 0.0 copy-start.6
  94.3 3.5 %fusion.15 = f32[1,1,120,3456]{3,2,1,0:T(8,128)S(1)} fusion(f32[]{:T(128)} %bitcast.1, f32[120,3456]{1,0:T(8,128)S(1)} %fusion.4, f32[1,1,120,3456]{3,2,1,0:T(8,128)S(1)} %copy-done.2, f32[1,1,120,3456]{3,2,1,0:T(8,128)S(1)} %copy-done.1, f32[1,1,120,3456]{3,2,1,0:T(8,128)} %copy-done.5, f32[1,1,120,3456]{3,2,1,0:T(8,128)S(1)} %copy-done, ...), kind=kLoop, calls=%fused_computation.20 | loop fusion | flops 7050240 | bytes 11612164 | tf_op jit(solution)/shard_map/broadcast_in_dim | solution.py:61
  97.8 0.0 copy-start.3
  97.8 2.6 %collective-permute-start.7 = (f32[1,1,120,3456]{3,2,1,0:T(8,128)S(1)}, f32[1,1,120,3456]{3,2,1,0:T(8,128)S(1)}, u32[]{:S(2)}, u32[]{:S(2)}) collective-permute-start(f32[1,1,120,3456]{3,2,1,0:T(8,128)S(1)} %fusion.15), channel_id=1, source_target_pairs={{4,0},{8,4},{12,8},{0,12},{5,1},{9,5},{13,9},{1,13},{6,2},{10,6},{... | collective-permute-start | bytes 4976648 | tf_op jit(solution)/shard_map/ppermute | solution.py:16
  100.4 0.0 collective-permute-start.6
  100.4 35.5 %collective-permute-start.3 = (f32[1,1]{1,0:T(1,128)}, f32[1,1]{1,0:T(1,128)}, u32[]{:S(2)}, u32[]{:S(2)}) collective-permute-start(f32[1,1]{1,0:T(1,128)} %div.50), channel_id=1, source_target_pairs={{4,0},{8,4},{12,8},{0,12},{5,1},{9,5},{13,9},{1,13},{6,2},{10,6},{... | collective-permute-start | bytes 20 | tf_op jit(solution)/shard_map/ppermute | solution.py:16
  135.9 0.7 collective-permute-start.2
  136.6 3.2 %collective-permute-done.2 = f32[1,1]{1,0:T(1,128)} collective-permute-done((f32[1,1]{1,0:T(1,128)}, f32[1,1]{1,0:T(1,128)}, u32[]{:S(2)}, u32[]{:S(2)}) %collective-permute-start.2) | collective-permute-done | bytes 36 | tf_op jit(solution)/shard_map/ppermute | solution.py:16
  141.0 0.0 collective-permute-done.7
  141.0 0.0 copy-start.8
  141.0 0.0 collective-permute-done.6
  141.1 0.0 copy-start.9
  141.1 0.0 copy-start.7
  141.1 1.8 %fusion.2 = f32[120,256]{1,0:T(8,128)S(1)} fusion(bf16[1,1,2,256,3456]{4,3,2,1,0:T(8,128)(2,1)S(1)} %copy-done.6, f32[1,1,120,3456]{3,2,1,0:T(8,128)S(1)} %collective-permute-done.7, f32[1,1,120,3456]{3,2,1,0:T(8,128)S(1)} %fusion.15, f32[1,1,120,3456]{3,2,1,0:T(8,128)S(1)} %collective-permute-done.6, f32[]{:T(128)} %bitcast), kind=kOutput, calls=%fused_computation.4 | convolution fusion | flops 1275678720 | bytes 6868996 | tf_op jit(solution)/shard_map/cf,tf->ct/dot_general | solution.py:50
  142.9 9.7 %all-gather.1 = f32[480,256]{1,0:T(8,128)S(1)} all-gather(f32[120,256]{1,0:T(8,128)S(1)} %fusion.2), channel_id=3, replica_groups=mesh['rx'=16,'ry'=4,'ma'=4] {'ma'}, dimensions={0}, use_global_device_ids=true | all-gather | bytes 614400 | tf_op jit(solution)/shard_map/all_gather | solution.py:53
  152.7 8.7 %fusion.21 = (f32[1,1,120,3456]{3,2,1,0:T(8,128)}, f32[1,1,120,3456]{3,2,1,0:T(8,128)}, f32[1,1,120,3456]{3,2,1,0:T(8,128)}) fusion(f32[120,3456]{1,0:T(8,128)S(1)} %fusion.4, f32[1,1,120,3456]{3,2,1,0:T(8,128)} %param.11, f32[1,1,120,3456]{3,2,1,0:T(8,128)} %param.10, f32[]{:T(128)} %bitcast, f32[1,1,120,3456]{3,2,1,0:T(8,128)} %copy-done.8, ...), kind=kOutput, calls=%fused_computation.29 | convolution fusion | flops 1284003840 | bytes 16946176 | tf_op jit(solution)/shard_map/ct,tf->cf/dot_general | solution.py:57
  (13 shorter events, 0.1 us)
Async XLA Ops:
  0.6 75.3 %collective-permute-start.4 = (f32[1,1,120,3456]{3,2,1,0:T(8,128)}, f32[1,1,120,3456]{3,2,1,0:T(8,128)S(1)}, u32[]{:S(2)}, u32[]{:S(2)}) collective-permute-start(f32[1,1,120,3456]{3,2,1,0:T(8,128)} %param.6), channel_id=1, source_target_pairs={{240,0},{0,16},{16,32},{32,48},{48,64},{64,80},{80,96},{96,112},{1... | collective-permute-start | bytes 4976648 | tf_op jit(solution)/shard_map/ppermute | solution.py:16
  2.8 73.1 %collective-permute-start.5 = (f32[1,1,120,3456]{3,2,1,0:T(8,128)}, f32[1,1,120,3456]{3,2,1,0:T(8,128)S(1)}, u32[]{:S(2)}, u32[]{:S(2)}) collective-permute-start(f32[1,1,120,3456]{3,2,1,0:T(8,128)} %param.6), channel_id=1, source_target_pairs={{16,0},{32,16},{48,32},{64,48},{80,64},{96,80},{112,96},{128,112},... | collective-permute-start | bytes 4976648 | tf_op jit(solution)/shard_map/ppermute | solution.py:16
  8.2 65.2 %collective-permute-start = (f32[1,1]{1,0:T(1,128)}, f32[1,1]{1,0:T(1,128)}, u32[]{:S(2)}, u32[]{:S(2)}) collective-permute-start(f32[1,1]{1,0:T(1,128)} %param.7), channel_id=1, source_target_pairs={{240,0},{0,16},{16,32},{32,48},{48,64},{64,80},{80,96},{96,112},{1... | collective-permute-start | bytes 20 | tf_op jit(solution)/shard_map/ppermute | solution.py:16
  8.2 67.1 %collective-permute-start.1 = (f32[1,1]{1,0:T(1,128)}, f32[1,1]{1,0:T(1,128)}, u32[]{:S(2)}, u32[]{:S(2)}) collective-permute-start(f32[1,1]{1,0:T(1,128)} %param.7), channel_id=1, source_target_pairs={{16,0},{32,16},{48,32},{64,48},{80,64},{96,80},{112,96},{128,112},... | collective-permute-start | bytes 20 | tf_op jit(solution)/shard_map/ppermute | solution.py:16
  76.0 5.0 %copy-start.4 = (f32[1,1,120,3456]{3,2,1,0:T(8,128)}, f32[1,1,120,3456]{3,2,1,0:T(8,128)S(1)}, u32[]{:S(2)}) copy-start(f32[1,1,120,3456]{3,2,1,0:T(8,128)S(1)} %collective-permute-done.4) | copy-start | bytes 4976644
  76.0 5.0 %copy-start.5 = (f32[1,1,120,3456]{3,2,1,0:T(8,128)}, f32[1,1,120,3456]{3,2,1,0:T(8,128)S(1)}, u32[]{:S(2)}) copy-start(f32[1,1,120,3456]{3,2,1,0:T(8,128)S(1)} %collective-permute-done.5) | copy-start | bytes 4976644
  76.0 18.3 %copy-start.2 = (f32[1,1,120,3456]{3,2,1,0:T(8,128)S(1)}, f32[1,1,120,3456]{3,2,1,0:T(8,128)}, u32[]{:S(2)}) copy-start(f32[1,1,120,3456]{3,2,1,0:T(8,128)} %param.10) | copy-start | bytes 4976644
  91.6 2.6 %copy-start = (f32[1,1,120,3456]{3,2,1,0:T(8,128)S(1)}, f32[1,1,120,3456]{3,2,1,0:T(8,128)}, u32[]{:S(2)}) copy-start(f32[1,1,120,3456]{3,2,1,0:T(8,128)} %param.6) | copy-start | bytes 4976644
  91.7 2.6 %copy-start.1 = (f32[1,1,120,3456]{3,2,1,0:T(8,128)S(1)}, f32[1,1,120,3456]{3,2,1,0:T(8,128)}, u32[]{:S(2)}) copy-start(f32[1,1,120,3456]{3,2,1,0:T(8,128)} %param.11) | copy-start | bytes 4976644
  94.3 46.8 %copy-start.6 = (bf16[1,1,2,256,3456]{4,3,2,1,0:T(8,128)(2,1)S(1)}, bf16[1,1,2,256,3456]{4,3,2,1,0:T(8,128)(2,1)}, u32[]{:S(2)}) copy-start(bf16[1,1,2,256,3456]{4,3,2,1,0:T(8,128)(2,1)} %param.8) | copy-start | bytes 10616836
  97.8 45.1 %copy-start.3 = (f32[1,1,120,3456]{3,2,1,0:T(8,128)}, f32[1,1,120,3456]{3,2,1,0:T(8,128)S(1)}, u32[]{:S(2)}) copy-start(f32[1,1,120,3456]{3,2,1,0:T(8,128)S(1)} %fusion.15) | copy-start | bytes 4976644
  97.8 43.2 %collective-permute-start.7 = (f32[1,1,120,3456]{3,2,1,0:T(8,128)S(1)}, f32[1,1,120,3456]{3,2,1,0:T(8,128)S(1)}, u32[]{:S(2)}, u32[]{:S(2)}) collective-permute-start(f32[1,1,120,3456]{3,2,1,0:T(8,128)S(1)} %fusion.15), channel_id=1, source_target_pairs={{4,0},{8,4},{12,8},{0,12},{5,1},{9,5},{13,9},{1,13},{6,2},{10,6},{... | collective-permute-start | bytes 4976648 | tf_op jit(solution)/shard_map/ppermute | solution.py:16
  100.4 40.7 %collective-permute-start.6 = (f32[1,1,120,3456]{3,2,1,0:T(8,128)S(1)}, f32[1,1,120,3456]{3,2,1,0:T(8,128)S(1)}, u32[]{:S(2)}, u32[]{:S(2)}) collective-permute-start(f32[1,1,120,3456]{3,2,1,0:T(8,128)S(1)} %fusion.15), channel_id=1, source_target_pairs={{12,0},{0,4},{4,8},{8,12},{13,1},{1,5},{5,9},{9,13},{14,2},{2,6},{... | collective-permute-start | bytes 4976648 | tf_op jit(solution)/shard_map/ppermute | solution.py:16
  100.4 40.1 %collective-permute-start.3 = (f32[1,1]{1,0:T(1,128)}, f32[1,1]{1,0:T(1,128)}, u32[]{:S(2)}, u32[]{:S(2)}) collective-permute-start(f32[1,1]{1,0:T(1,128)} %div.50), channel_id=1, source_target_pairs={{4,0},{8,4},{12,8},{0,12},{5,1},{9,5},{13,9},{1,13},{6,2},{10,6},{... | collective-permute-start | bytes 20 | tf_op jit(solution)/shard_map/ppermute | solution.py:16
  135.9 3.9 %collective-permute-start.2 = (f32[1,1]{1,0:T(1,128)}, f32[1,1]{1,0:T(1,128)}, u32[]{:S(2)}, u32[]{:S(2)}) collective-permute-start(f32[1,1]{1,0:T(1,128)} %div.50), channel_id=1, source_target_pairs={{12,0},{0,4},{4,8},{8,12},{13,1},{1,5},{5,9},{9,13},{14,2},{2,6},{... | collective-permute-start | bytes 20 | tf_op jit(solution)/shard_map/ppermute | solution.py:16
  141.0 1.9 %copy-start.8 = (f32[1,1,120,3456]{3,2,1,0:T(8,128)}, f32[1,1,120,3456]{3,2,1,0:T(8,128)S(1)}, u32[]{:S(2)}) copy-start(f32[1,1,120,3456]{3,2,1,0:T(8,128)S(1)} %collective-permute-done.7) | copy-start | bytes 4976644
  141.1 1.9 %copy-start.9 = (f32[1,1,120,3456]{3,2,1,0:T(8,128)}, f32[1,1,120,3456]{3,2,1,0:T(8,128)S(1)}, u32[]{:S(2)}) copy-start(f32[1,1,120,3456]{3,2,1,0:T(8,128)S(1)} %collective-permute-done.6) | copy-start | bytes 4976644
  141.1 11.6 %copy-start.7 = (f32[1,1,2,120,256]{4,3,2,1,0:T(8,128)S(1)}, f32[1,1,2,120,256]{4,3,2,1,0:T(8,128)}, u32[]{:S(2)}) copy-start(f32[1,1,2,120,256]{4,3,2,1,0:T(8,128)} %param.9) | copy-start | bytes 737284
